TPU v7x, 32 devices: a whole 2x2x4 slice. The times are simulated.
32 devices in a mesh: groups: 2 (over y), team: 4 (over z), rep: 4 (over x, core).
Axes of the slice: x: 2, y: 2, z: 4, core: 2. Of those that a mesh axis runs over, the one named last changes fastest.
Arguments:
- omega_rows: float32 [128, 32768], P(('groups', 'team'), 'rep'), parts along dimension 0, as said below
- covariance_columns: float32 [32768, 2048], P('rep', ('groups', 'team')), parts along dimension 1, may hold values from -0.03125 to 0.03125
- tile_offsets: int32 [8], P(('groups', 'team')), parts along dimension 0, may hold values from 0 to 32512, as said below
Outputs:
- new_omega: float32 [64, 2048], P('rep', ('groups', 'team')), parts along dimension 1
There are 2 independent parts, one for each index of `groups`. A program takes and returns all parts, laid end to end along the dimension named above; each array names one. Nothing has to cross between parts.
Inputs may be any that keep to these rules, and one draw needn't show every extreme that they name: `tile_offsets`: distinct multiples of 256; both 0 and 32512 occur. `omega_rows`: entries with column equal to row lie in 1 to 2.
All inputs are finite; a program needn't handle non-finite values.
Results may differ from a plain program's by a relative error of at most 0.0003.
Values sent between devices are 32-bit elements; how exact they have to be, the bound alone decides.
A program may use at most 64 MiB of HBM per device.

v0:
```python
import jax
import jax.numpy as jnp
from jax import lax
from jax.sharding import PartitionSpec as P

step_size = 0.5
penalty = 0.1


def shifted(array, axis, by):
    devices = lax.axis_size(axis)
    return lax.ppermute(array, axis, [(i, (i + by) % devices) for i in range(devices)])


def from_root(array, axis, root):
    mine = lax.axis_index(axis) == root
    return lax.psum(jnp.where(mine, array, jnp.zeros_like(array)), axis)


def per_device(omega_rows, covariance_columns, tile_offsets):
    team_count = lax.axis_size("team")
    rep_count = lax.axis_size("rep")
    team_index = lax.axis_index("team")
    rep_index = lax.axis_index("rep")
    block_rows, part_width = omega_rows.shape
    tile_width = covariance_columns.shape[1]
    all_rows = block_rows * team_count
    rows_share = all_rows // rep_count
    offset = tile_offsets[0]
    owner = offset // part_width
    inside = jnp.clip(offset - rep_index * part_width, 0, part_width - tile_width)

    def place(collected, block, source):
        first = source * block_rows
        return lax.dynamic_update_slice_in_dim(collected, block, first, 0)

    empty = jnp.zeros((all_rows, part_width), jnp.float32)

    def advance(shift_count, carry):
        block, collected = carry
        block = shifted(block, "team", 1)
        source = (team_index - shift_count) % team_count
        return (block, place(collected, block, source))

    final = lax.fori_loop(
        1, team_count, advance, (omega_rows, place(empty, omega_rows, team_index))
    )
    collected = final[1]
    partial_value = jnp.dot(
        collected,
        covariance_columns,
        preferred_element_type=jnp.float32,
        precision=lax.Precision.HIGHEST,
    )
    values = lax.dynamic_slice_in_dim(collected, inside, tile_width, 1)
    summed = lax.psum_scatter(partial_value, "rep", scatter_dimension=0, tiled=True)
    everyone = from_root(values, "rep", owner)
    current = lax.dynamic_slice_in_dim(everyone, rep_index * rows_share, rows_share, 0)
    global_rows = rep_index * rows_share + jnp.arange(rows_share, dtype=jnp.int32)
    global_cols = offset + jnp.arange(tile_width, dtype=jnp.int32)
    diagonal = global_rows[:, None] == global_cols[None, :]
    safe = jnp.where(diagonal, current, jnp.float32(1.0))
    gradient = summed - jnp.where(diagonal, 1.0 / safe, jnp.float32(0.0))
    moved = current - step_size * gradient
    shrunk = jnp.sign(moved) * jnp.maximum(jnp.abs(moved) - step_size * penalty, 0.0)
    return jnp.where(diagonal, moved, shrunk)


def solution(mesh):
    in_specs = (P(("groups", "team"), "rep"), P("rep", ("groups", "team")), P(("groups", "team")))
    out_specs = P("rep", ("groups", "team"))
    return jax.shard_map(
        per_device, mesh=mesh, in_specs=in_specs, out_specs=out_specs, check_vma=False
    )
```

profile of v0, /device:TPU:0, one launch (start us, length us, event | category | flops | bytes accessed | tf_op | source)
XLA Modules:
  0.0 114.8 jit_solution(6271310564918737601)
XLA Ops:
  6.5 0.0 all-reduce.2.cloned.1.call-start
  6.5 1.0 copy.18
  8.3 0.1 broadcast_in_dim.13
  8.5 46.3 %while.17 = (s32[]{:T(128)}, f32[16,8192]{1,0:T(8,128)S(1)}, f32[64,8192]{1,0:T(8,128)S(1)}, s32[]{:T(128)}, s32[]{:T(128)}, /*index=5*/s32[]{:T(128)}, s32[]{:T(128)}, s32[]{:T(128)}, s32[]{:T(128)}, s32[]{:T(128)}) while((s32[]{:T(128)}, f32[16,8192]{1,0:T(8,128)S(1)}, f32[64,8192]{1,0:T(8,128)S(1)}, s32[]{:T(128)}, s32[]{:T(128)}, ...), condition=%wide.region_1.2_spmd, body=%wide.region_0.1_spmd.sunk | while | flops 18 | bytes 4194616 | solution.py:45
  8.5 3.1 %collective-permute-start = (f32[16,8192]{1,0:T(8,128)S(1)}, f32[16,8192]{1,0:T(8,128)S(1)}, u32[]{:S(2)}, u32[]{:S(2)}) collective-permute-start(f32[16,8192]{1,0:T(8,128)S(1)} %get-tuple-element.161), channel_id=1, source_target_pairs={{0,4},{4,8},{8,12},{12,0},{1,5},{5,9},{9,13},{13,1},{2,6},{6,10},{... | collective-permute-start | bytes 1572872 | tf_op jit(solution)/shard_map/while/body/eval_jaxpr/ppermute | solution.py:12
  11.5 13.9 %collective-permute-done = f32[16,8192]{1,0:T(8,128)S(1)} collective-permute-done((f32[16,8192]{1,0:T(8,128)S(1)}, f32[16,8192]{1,0:T(8,128)S(1)}, u32[]{:S(2)}, u32[]{:S(2)}) %collective-permute-start) | collective-permute-done | bytes 524320 | tf_op jit(solution)/shard_map/while/body/eval_jaxpr/ppermute | solution.py:12
  25.6 0.1 collective-permute-start
  25.7 14.9 %collective-permute-done = f32[16,8192]{1,0:T(8,128)S(1)} collective-permute-done((f32[16,8192]{1,0:T(8,128)S(1)}, f32[16,8192]{1,0:T(8,128)S(1)}, u32[]{:S(2)}, u32[]{:S(2)}) %collective-permute-start) | collective-permute-done | bytes 524320 | tf_op jit(solution)/shard_map/while/body/eval_jaxpr/ppermute | solution.py:12
  40.7 0.1 collective-permute-start
  40.7 13.9 %collective-permute-done = f32[16,8192]{1,0:T(8,128)S(1)} collective-permute-done((f32[16,8192]{1,0:T(8,128)S(1)}, f32[16,8192]{1,0:T(8,128)S(1)}, u32[]{:S(2)}, u32[]{:S(2)}) %collective-permute-start) | collective-permute-done | bytes 524320 | tf_op jit(solution)/shard_map/while/body/eval_jaxpr/ppermute | solution.py:12
  54.8 0.7 dynamic-slice_select_fusion
  55.5 0.0 all-reduce.2.cloned.1.call-update
  55.5 0.0 reduce-scatter.2.cloned.1.call-start
  55.6 7.3 %fusion.4 = f32[64,256]{1,0:T(8,128)} fusion(f32[64,8192]{1,0:T(8,128)S(1)} %get-tuple-element.116, f32[8192,256]{1,0:T(8,128)} %param.6), kind=kOutput, calls=%fused_computation.12 | convolution fusion | flops 1610612736 | bytes 10551296 | tf_op jit(solution)/shard_map/dot_general | solution.py:49
  62.9 0.0 reduce-scatter.2.cloned.1.call-update
  63.0 21.5 %all-reduce.2.cloned.1.call-done = f32[64,256]{1,0:T(8,128)} async-done(((f32[64,256]{1,0:T(8,128)}), f32[64,256]{1,0:T(8,128)}) %all-reduce.2.cloned.1.call-update) | async-done | bytes 65552 | tf_op jit(solution)/shard_map/psum | solution.py:17
  84.5 22.0 %reduce-scatter.2.cloned.1.call-done = f32[16,256]{1,0:T(8,128)} async-done(((f32[64,256]{1,0:T(8,128)}), f32[16,256]{1,0:T(8,128)}) %reduce-scatter.2.cloned.1.call-update) | async-done | bytes 16400 | tf_op jit(solution)/shard_map/reduce_scatter | solution.py:56
  106.5 1.4 %compare_select_fusion = f32[16,256]{1,0:T(8,128)} fusion(f32[16,256]{1,0:T(8,128)} %reduce-scatter.2.cloned.1.call-done, f32[64,256]{1,0:T(8,128)} %all-reduce.2.cloned.1.call-done, s32[]{:T(128)S(6)} %select_n.64, s32[256]{0:T(256)S(1)} %iota_add_fusion, s32[16]{0:T(128)S(1)} %iota_add_fusion.1), kind=kLoop, calls=%fused_computation.2 | loop fusion | flops 53248 | bytes 50244 | tf_op jit(solution)/shard_map/jit(_where)/select_n | solution.py:66
  (9 shorter events, 0.3 us)
Async XLA Ops:
  6.5 78.0 %all-reduce.2.cloned.1.call-start = ((), (), s32[]{:S(2)}) async-start(), calls=%async_computation.1 | async-start | bytes 131072 | tf_op jit(solution)/shard_map/psum | solution.py:17
  8.5 17.0 %collective-permute-start = (f32[16,8192]{1,0:T(8,128)S(1)}, f32[16,8192]{1,0:T(8,128)S(1)}, u32[]{:S(2)}, u32[]{:S(2)}) collective-permute-start(f32[16,8192]{1,0:T(8,128)S(1)} %get-tuple-element.161), channel_id=1, source_target_pairs={{0,4},{4,8},{8,12},{12,0},{1,5},{5,9},{9,13},{13,1},{2,6},{6,10},{... | collective-permute-start | bytes 1572872 | tf_op jit(solution)/shard_map/while/body/eval_jaxpr/ppermute | solution.py:12
  25.6 15.0 %collective-permute-start = (f32[16,8192]{1,0:T(8,128)S(1)}, f32[16,8192]{1,0:T(8,128)S(1)}, u32[]{:S(2)}, u32[]{:S(2)}) collective-permute-start(f32[16,8192]{1,0:T(8,128)S(1)} %get-tuple-element.161), channel_id=1, source_target_pairs={{0,4},{4,8},{8,12},{12,0},{1,5},{5,9},{9,13},{13,1},{2,6},{6,10},{... | collective-permute-start | bytes 1572872 | tf_op jit(solution)/shard_map/while/body/eval_jaxpr/ppermute | solution.py:12
  40.7 14.0 %collective-permute-start = (f32[16,8192]{1,0:T(8,128)S(1)}, f32[16,8192]{1,0:T(8,128)S(1)}, u32[]{:S(2)}, u32[]{:S(2)}) collective-permute-start(f32[16,8192]{1,0:T(8,128)S(1)} %get-tuple-element.161), channel_id=1, source_target_pairs={{0,4},{4,8},{8,12},{12,0},{1,5},{5,9},{9,13},{13,1},{2,6},{6,10},{... | collective-permute-start | bytes 1572872 | tf_op jit(solution)/shard_map/while/body/eval_jaxpr/ppermute | solution.py:12
  55.5 51.0 %reduce-scatter.2.cloned.1.call-start = ((), (), s32[]{:S(2)}) async-start(), calls=%async_computation.2 | async-start | bytes 81920 | tf_op jit(solution)/shard_map/reduce_scatter | solution.py:56
Sparse Core Ops, SparseCore 0:
  55.7 28.7 all-reduce.1
  87.0 19.4 reduce-scatter.1
where the time goes:
time: 115 us
  waiting for transfers between devices  86.4 us (75%)
  between operations  14.1 us (12%)
  matrix products  7.33 us (6%)
  starting transfers between devices  3.24 us (3%)
  other arithmetic  2.16 us (2%)
  local copies, waits for them, and re-layouts  1.45 us (1%)
    ppermute x3, waiting for transfers between devices, shifted(): lax.ppermute(array, axis, [(i, (i + by) % devices) for i in range(devices)])  42.8 us
    reduce_scatter x1, waiting for transfers between devices, per_device(): lax.psum_scatter(partial_value, 'rep', scatter_dimension=0, tiled=True)  22 us
    psum x1, waiting for transfers between devices, from_root(): return lax.psum(jnp.where(mine, array, jnp.zeros_like(array)), axis)  21.5 us
    dot_general x1, matrix products, per_device(): jnp.dot(collected, covariance_columns, preferred_element_type=jnp.float32...  7.33 us
    ppermute x3, starting transfers between devices, shifted(): lax.ppermute(array, axis, [(i, (i + by) % devices) for i in range(devices)])  3.19 us
  transfers between devices with their start and end apart: 5, of which 5 were waited for; matrix products, arithmetic and copies ran while one was open for 6% of the time, Pallas kernels for 0%

commit v1 on v0

--- a/solution.py
+++ b/solution.py
@@ -5,6 +5,7 @@
 
 step_size = 0.5
 penalty = 0.1
+solve_widths_for = lambda arr_in, bus_axis: jnp.sum(lax.all_gather(arr_in, bus_axis), 0)
 
 
 def shifted(array, axis, by):
@@ -14,7 +15,7 @@
 
 def from_root(array, axis, root):
     mine = lax.axis_index(axis) == root
-    return lax.psum(jnp.where(mine, array, jnp.zeros_like(array)), axis)
+    return solve_widths_for(jnp.where(mine, array, jnp.zeros_like(array)), axis)
 
 
 def per_device(omega_rows, covariance_columns, tile_offsets):

time: 115 us -> 87.3 us (0.76)
  waiting for transfers between devices: 86.4 us -> 53.5 us
  blocking collectives: 0 us -> 5.79 us
    psum x1 -> x0, waiting for transfers between devices: 21.5 us -> none  [from_root(): return lax.psum(jnp.where(mine, array, jnp.zeros_like(array)), axis)]
    reduce_scatter x1, waiting for transfers between devices: 22 us -> 10.7 us  [per_device(): lax.psum_scatter(partial_value, 'rep', scatter_dimension=0, tiled=True)]
    all_gather x0 -> x1, blocking collectives: none -> 5.79 us  [lax.all_gather(arr_in, bus_axis)]
  transfers between devices with their start and end apart: 5 -> 4, of which waited for: 5 -> 4; matrix products, arithmetic and copies ran while one was open for 6% -> 0% of each run, Pallas kernels for 0% -> 0%
where the time goes in v1:
time: 87.3 us; the launch traced here: 87 us
  waiting for transfers between devices  53.5 us (61%)
  between operations  14.1 us (16%)
  matrix products  7.32 us (8%)
  blocking collectives  5.79 us (7%)
  starting transfers between devices  3.2 us (4%)
  other arithmetic  1.52 us (2%)
  local copies, waits for them, and re-layouts  1.45 us (2%)
    ppermute x3, waiting for transfers between devices, shifted(): lax.ppermute(array, axis, [(i, (i + by) % devices) for i in range(devices)])  42.8 us
    reduce_scatter x1, waiting for transfers between devices, per_device(): lax.psum_scatter(partial_value, 'rep', scatter_dimension=0, tiled=True)  10.7 us
    dot_general x1, matrix products, per_device(): jnp.dot(collected, covariance_columns, preferred_element_type=jnp.float32...  7.32 us
    all_gather x1, blocking collectives, lax.all_gather(arr_in, bus_axis)  5.79 us
    ppermute x3, starting transfers between devices, shifted(): lax.ppermute(array, axis, [(i, (i + by) % devices) for i in range(devices)])  3.19 us
  transfers between devices with their start and end apart: 4, of which 4 were waited for; matrix products, arithmetic and copies ran while one was open for 0% of the time, Pallas kernels for 0%

profile of v1, /device:TPU:0, one launch (start us, length us, event | category | flops | bytes accessed | tf_op | source)
XLA Modules:
  0.0 87.0 jit_solution(14651481155782846844)
XLA Ops:
  6.5 0.0 reduce-scatter.2.cloned.1.call-start
  6.5 1.0 %copy.17 = f32[16,8192]{1,0:T(8,128)S(1)} copy(f32[16,8192]{1,0:T(8,128)} %param.5) | data formatting | bytes 1048576
  7.6 0.1 broadcast_in_dim.13
  7.8 46.3 %while.17 = (s32[]{:T(128)}, f32[16,8192]{1,0:T(8,128)S(1)}, f32[64,8192]{1,0:T(8,128)S(1)}, s32[]{:T(128)}, s32[]{:T(128)}, /*index=5*/s32[]{:T(128)}, s32[]{:T(128)}, s32[]{:T(128)}, s32[]{:T(128)}, s32[]{:T(128)}) while((s32[]{:T(128)}, f32[16,8192]{1,0:T(8,128)S(1)}, f32[64,8192]{1,0:T(8,128)S(1)}, s32[]{:T(128)}, s32[]{:T(128)}, ...), condition=%wide.region_1.2_spmd, body=%wide.region_0.1_spmd.sunk | while | flops 18 | bytes 4194616 | solution.py:46
  7.8 3.1 %collective-permute-start = (f32[16,8192]{1,0:T(8,128)S(1)}, f32[16,8192]{1,0:T(8,128)S(1)}, u32[]{:S(2)}, u32[]{:S(2)}) collective-permute-start(f32[16,8192]{1,0:T(8,128)S(1)} %get-tuple-element.161), channel_id=1, source_target_pairs={{0,4},{4,8},{8,12},{12,0},{1,5},{5,9},{9,13},{13,1},{2,6},{6,10},{... | collective-permute-start | bytes 1572872 | tf_op jit(solution)/shard_map/while/body/eval_jaxpr/ppermute | solution.py:13
  10.9 13.9 %collective-permute-done = f32[16,8192]{1,0:T(8,128)S(1)} collective-permute-done((f32[16,8192]{1,0:T(8,128)S(1)}, f32[16,8192]{1,0:T(8,128)S(1)}, u32[]{:S(2)}, u32[]{:S(2)}) %collective-permute-start) | collective-permute-done | bytes 524320 | tf_op jit(solution)/shard_map/while/body/eval_jaxpr/ppermute | solution.py:13
  24.9 0.1 collective-permute-start
  25.0 14.9 %collective-permute-done = f32[16,8192]{1,0:T(8,128)S(1)} collective-permute-done((f32[16,8192]{1,0:T(8,128)S(1)}, f32[16,8192]{1,0:T(8,128)S(1)}, u32[]{:S(2)}, u32[]{:S(2)}) %collective-permute-start) | collective-permute-done | bytes 524320 | tf_op jit(solution)/shard_map/while/body/eval_jaxpr/ppermute | solution.py:13
  40.0 0.1 collective-permute-start
  40.1 13.9 %collective-permute-done = f32[16,8192]{1,0:T(8,128)S(1)} collective-permute-done((f32[16,8192]{1,0:T(8,128)S(1)}, f32[16,8192]{1,0:T(8,128)S(1)}, u32[]{:S(2)}, u32[]{:S(2)}) %collective-permute-start) | collective-permute-done | bytes 524320 | tf_op jit(solution)/shard_map/while/body/eval_jaxpr/ppermute | solution.py:13
  54.1 7.3 %fusion.4 = f32[64,256]{1,0:T(8,128)} fusion(f32[64,8192]{1,0:T(8,128)S(1)} %get-tuple-element.116, f32[8192,256]{1,0:T(8,128)} %param.6), kind=kOutput, calls=%fused_computation.12 | convolution fusion | flops 1610612736 | bytes 10551296 | tf_op jit(solution)/shard_map/dot_general | solution.py:50
  61.4 0.0 reduce-scatter.2.cloned.1.call-update
  62.1 0.1 dynamic-slice_select_fusion
  62.2 5.8 %all-gather = f32[256,256]{1,0:T(8,128)S(1)} all-gather(f32[64,256]{1,0:T(8,128)S(1)} %dynamic-slice_select_fusion), channel_id=2, replica_groups=mesh['groups'=2,'team'=4,'rep'=4] {'rep'}, dimensions={0}, use_global_device_ids=true | all-gather | bytes 327680 | tf_op jit(solution)/shard_map/all_gather | solution.py:8
  68.1 10.7 %reduce-scatter.2.cloned.1.call-done = f32[16,256]{1,0:T(8,128)} async-done(((f32[64,256]{1,0:T(8,128)}), f32[16,256]{1,0:T(8,128)}) %reduce-scatter.2.cloned.1.call-update) | async-done | bytes 16400 | tf_op jit(solution)/shard_map/reduce_scatter | solution.py:57
  78.7 1.4 %compare_select_fusion = f32[16,256]{1,0:T(8,128)} fusion(f32[16,256]{1,0:T(8,128)} %reduce-scatter.2.cloned.1.call-done, f32[64,256]{1,0:T(8,128)S(1)} %reduce_sum.9, s32[]{:T(128)S(6)} %select_n.64, s32[256]{0:T(256)S(1)} %iota_add_fusion, s32[16]{0:T(128)S(1)} %iota_add_fusion.1), kind=kLoop, calls=%fused_computation.2 | loop fusion | flops 53248 | bytes 50244 | tf_op jit(solution)/shard_map/jit(_where)/select_n | solution.py:67
  (10 shorter events, 0.3 us)
Async XLA Ops:
  6.5 72.2 %reduce-scatter.2.cloned.1.call-start = ((), (), s32[]{:S(2)}) async-start(), calls=%async_computation.1 | async-start | bytes 81920 | tf_op jit(solution)/shard_map/reduce_scatter | solution.py:57
  7.8 17.0 %collective-permute-start = (f32[16,8192]{1,0:T(8,128)S(1)}, f32[16,8192]{1,0:T(8,128)S(1)}, u32[]{:S(2)}, u32[]{:S(2)}) collective-permute-start(f32[16,8192]{1,0:T(8,128)S(1)} %get-tuple-element.161), channel_id=1, source_target_pairs={{0,4},{4,8},{8,12},{12,0},{1,5},{5,9},{9,13},{13,1},{2,6},{6,10},{... | collective-permute-start | bytes 1572872 | tf_op jit(solution)/shard_map/while/body/eval_jaxpr/ppermute | solution.py:13
  24.9 15.0 %collective-permute-start = (f32[16,8192]{1,0:T(8,128)S(1)}, f32[16,8192]{1,0:T(8,128)S(1)}, u32[]{:S(2)}, u32[]{:S(2)}) collective-permute-start(f32[16,8192]{1,0:T(8,128)S(1)} %get-tuple-element.161), channel_id=1, source_target_pairs={{0,4},{4,8},{8,12},{12,0},{1,5},{5,9},{9,13},{13,1},{2,6},{6,10},{... | collective-permute-start | bytes 1572872 | tf_op jit(solution)/shard_map/while/body/eval_jaxpr/ppermute | solution.py:13
  40.0 14.0 %collective-permute-start = (f32[16,8192]{1,0:T(8,128)S(1)}, f32[16,8192]{1,0:T(8,128)S(1)}, u32[]{:S(2)}, u32[]{:S(2)}) collective-permute-start(f32[16,8192]{1,0:T(8,128)S(1)} %get-tuple-element.161), channel_id=1, source_target_pairs={{0,4},{4,8},{8,12},{12,0},{1,5},{5,9},{9,13},{13,1},{2,6},{6,10},{... | collective-permute-start | bytes 1572872 | tf_op jit(solution)/shard_map/while/body/eval_jaxpr/ppermute | solution.py:13
Sparse Core Ops, SparseCore 0:
  61.6 17.1 reduce-scatter.1
